TPU v7x, 512 devices: a whole 4x4x16 slice. The times are simulated.
512 devices in a mesh: dp: 8 (over y, x_hi), expert: 64 (over z, x_lo, core).
Axes of the slice: x: 4 (x_hi: 2, x_lo: 2; x = x_hi * 2 + x_lo), y: 4, z: 16, core: 2. Of those that a mesh axis runs over, the one named last changes fastest.
Arguments:
- tokens: bfloat16 [32768, 2048], P(('dp', 'expert')), parts along dimension 0, may hold values from -6 to 6
- gate_weight: bfloat16 [2048, 16384], P(None, 'expert'), may hold values from -0.125 to 0.125
- up_weight: bfloat16 [2048, 16384], P(None, 'expert'), may hold values from -0.125 to 0.125
- down_weight: bfloat16 [16384, 2048], P('expert'), may hold values from -0.1875 to 0.1875
- route_ids: int32 [32768, 8], P(('dp', 'expert')), parts along dimension 0, may hold values from 0 to 15, all different within a row
- route_weight: float32 [32768, 8], P(('dp', 'expert')), parts along dimension 0, may hold values from 0.2 to 2
Outputs:
- layer_out: bfloat16 [32768, 2048], P(('dp', 'expert')), parts along dimension 0
There are 8 independent parts, one for each index of `dp`. A program takes and returns all parts, laid end to end along the dimension named above; an argument that names none is the same for every part. Nothing has to cross between parts.
Inputs may be any that keep to these rules, and one draw needn't show every extreme that they name: `route_ids`: each token names 8 different experts.
All inputs are finite; a program needn't handle non-finite values.
Results may differ from a plain program's by a relative error of at most 0.0072.
Values may be sent and summed in bfloat16 or wider, within the bound.
A program may use at most 128 MiB of HBM per device.

v0:
```python
import jax
import jax.numpy as jnp
from jax import lax
from jax.sharding import PartitionSpec as P

EXPERTS = 16
CAP = 32


def expert_rows(flat_rows, gate_part, up_part, down_part):
    gate_act = jnp.dot(flat_rows, gate_part, preferred_element_type=jnp.float32)
    up_act = jnp.dot(flat_rows, up_part, preferred_element_type=jnp.float32)
    hidden = (jax.nn.silu(gate_act) * up_act).astype(jnp.bfloat16)
    return jnp.dot(hidden, down_part, preferred_element_type=jnp.float32).astype(jnp.bfloat16)


def in_blocks(arrived, gate_part, up_part, down_part):
    sources, slot_count, features = arrived.shape
    per_block = max(1, min(sources, 512 // max(1, slot_count)))
    while sources % per_block != 0:
        per_block = per_block - 1
    blocks = arrived.reshape(sources // per_block, per_block * slot_count, features)

    def one_block(flat_rows):
        return expert_rows(flat_rows, gate_part, up_part, down_part)

    results = lax.map(one_block, blocks)
    return results.reshape(sources, slot_count, features)


def tree_parts(parts):
    width = parts.shape[1]
    while width > 1:
        shaped = parts.reshape(parts.shape[0], width // 2, 2, parts.shape[2], parts.shape[3])
        parts = (shaped[:, :, 0].astype(jnp.float32) + shaped[:, :, 1].astype(jnp.float32)).astype(
            jnp.bfloat16
        )
        parts = lax.optimization_barrier(parts)
        width = width // 2
    return parts[:, 0].astype(jnp.float32)


def on_device(tokens, gate_weight, up_weight, down_weight, route_ids, route_weight):
    split_count = lax.axis_size("expert") // EXPERTS
    capacity = CAP
    features = tokens.shape[1]
    labels = jnp.arange(EXPERTS, dtype=jnp.int32)
    matches = route_ids[:, :, None] == labels[None, None, :]
    counts = jnp.sum(matches.astype(jnp.int32), axis=1)
    raw_shares = jnp.sum(jnp.where(matches, route_weight[:, :, None], jnp.float32(0.0)), axis=1)
    places = jnp.cumsum(counts, axis=0) - counts
    kept_slot = (counts == 1) & (places < capacity)
    shares = jnp.where(kept_slot, raw_shares, jnp.float32(0.0))
    slot_ids = jnp.arange(capacity, dtype=jnp.int32)
    chosen = kept_slot[:, :, None] & (places[:, :, None] == slot_ids[None, None, :])
    packed = jnp.einsum(
        "tec,td->ecd", chosen.astype(jnp.bfloat16), tokens, preferred_element_type=jnp.float32
    ).astype(jnp.bfloat16)
    outgoing = jnp.broadcast_to(packed[:, None], (EXPERTS, split_count, capacity, features))
    outgoing = outgoing.reshape(EXPERTS * split_count, capacity, features)
    returned = lax.all_to_all(
        in_blocks(
            lax.all_to_all(outgoing, "expert", split_axis=0, concat_axis=0, tiled=True),
            gate_weight,
            up_weight,
            down_weight,
        ),
        "expert",
        split_axis=0,
        concat_axis=0,
        tiled=True,
    )
    summed = tree_parts(returned.reshape(EXPERTS, split_count, capacity, features))
    weights = chosen.astype(jnp.float32) * shares[:, :, None]
    layer_out = jnp.einsum("tec,ecd->td", weights, summed, precision=lax.Precision.HIGHEST)
    return layer_out.astype(jnp.bfloat16)


def solution(mesh):
    return jax.shard_map(
        on_device,
        mesh=mesh,
        in_specs=(
            P(("dp", "expert"), None),
            P(None, "expert"),
            P(None, "expert"),
            P("expert", None),
            P(("dp", "expert"), None),
            P(("dp", "expert"), None),
        ),
        out_specs=P(("dp", "expert"), None),
        check_vma=False,
    )
```

profile of v0, /device:TPU:1, one launch (start us, length us, event | category | flops | bytes accessed | tf_op | source)
XLA Modules:
  0.0 805.9 jit_solution(500031062860425178)
XLA Ops:
  0.0 0.0 copy-start
  0.0 0.7 convert_reduce_fusion
  0.8 0.7 select_reduce_fusion
  1.5 0.1 copy.17
  1.6 0.1 copy.22
  1.6 0.1 reduce_window_sum.11
  1.8 0.1 copy.20
  1.8 0.1 copy.21
  1.9 0.0 copy-done
  1.9 0.7 convolution_convert_fusion.1
  2.6 4.3 broadcast_in_dim.40
  6.9 0.0 copy-start.1
  6.9 18.5 %all-to-all-start = ((bf16[64,32,2048]{2,1,0:T(8,128)(2,1)}), bf16[64,32,2048]{2,1,0:T(8,128)(2,1)}, u32[]{:S(2)}, u32[]{:S(2)}) async-start(bf16[64,32,2048]{2,1,0:T(8,128)(2,1)} %bitcast.49), calls=%async_computation | async-start | bytes 16777216 | tf_op jit(solution)/shard_map/all_to_all | solution.py:63
  25.4 364.1 %all-to-all-done = bf16[64,32,2048]{2,1,0:T(8,128)(2,1)} async-done(((bf16[64,32,2048]{2,1,0:T(8,128)(2,1)}), bf16[64,32,2048]{2,1,0:T(8,128)(2,1)}, u32[]{:S(2)}, u32[]{:S(2)}) %all-to-all-start) | async-done | bytes 8388640 | tf_op jit(solution)/shard_map/all_to_all | solution.py:63
  389.6 0.0 copy-done.1
  389.6 0.0 copy-done.2
  389.6 0.0 copy-done.3
  389.6 33.7 %while.10 = (s32[]{:T(128)}, bf16[4,512,2048]{2,1,0:T(8,128)(2,1)}, bf16[4,512,2048]{2,1,0:T(8,128)(2,1)}, bf16[2048,256]{1,0:T(8,128)(2,1)S(1)}, bf16[2048,256]...) while((s32[]{:T(128)}, bf16[4,512,2048]{2,1,0:T(8,128)(2,1)}, ...), condition=%wide.region_4.5_spmd, body=%wide.region_3.4_spmd.sunk | while | flops 1612447744 | bytes 10486873 | solution.py:27
  389.6 3.1 fusion.57
  392.7 5.4 fusion.58
  398.1 3.1 fusion.57
  401.2 5.3 fusion.58
  406.5 3.1 fusion.57
  409.6 5.3 fusion.58
  414.9 3.1 fusion.57
  418.0 5.3 fusion.58
  423.3 12.1 %all-to-all-start.1 = ((bf16[64,32,2048]{2,1,0:T(8,128)(2,1)}), bf16[64,32,2048]{2,1,0:T(8,128)(2,1)}, u32[]{:S(2)}, u32[]{:S(2)}) async-start(bf16[64,32,2048]{2,1,0:T(8,128)(2,1)} %bitcast.51), calls=%async_computation.1 | async-start | bytes 16777216 | tf_op jit(solution)/shard_map/all_to_all | solution.py:61
  435.3 0.1 copy.23
  435.4 363.3 %all-to-all-done.1 = bf16[64,32,2048]{2,1,0:T(8,128)(2,1)} async-done(((bf16[64,32,2048]{2,1,0:T(8,128)(2,1)}), bf16[64,32,2048]{2,1,0:T(8,128)(2,1)}, u32[]{:S(2)}, u32[]{:S(2)}) %all-to-all-start.1) | async-done | bytes 8388640 | tf_op jit(solution)/shard_map/all_to_all | solution.py:61
  798.7 4.3 fusion.26
  803.0 0.9 fusion.28
  803.9 2.0 fusion.27
  (4 shorter events, 0.0 us)
Async XLA Ops:
  0.0 1.9 copy-start
  6.9 382.7 %copy-start.1 = (bf16[2048,256]{1,0:T(8,128)(2,1)S(1)}, bf16[2048,256]{1,0:T(8,128)(2,1)}, u32[]{:S(2)}) copy-start(bf16[2048,256]{1,0:T(8,128)(2,1)} %param.9) | copy-start | bytes 3145732
  6.9 382.7 %copy-start.2 = (bf16[2048,256]{1,0:T(8,128)(2,1)S(1)}, bf16[2048,256]{1,0:T(8,128)(2,1)}, u32[]{:S(2)}) copy-start(bf16[2048,256]{1,0:T(8,128)(2,1)} %param.10) | copy-start | bytes 3145732
  6.9 382.7 %copy-start.3 = (bf16[256,2048]{1,0:T(8,128)(2,1)S(1)}, bf16[256,2048]{1,0:T(8,128)(2,1)}, u32[]{:S(2)}) copy-start(bf16[256,2048]{1,0:T(8,128)(2,1)} %param.11) | copy-start | bytes 3145732
  6.9 382.7 %all-to-all-start = ((bf16[64,32,2048]{2,1,0:T(8,128)(2,1)}), bf16[64,32,2048]{2,1,0:T(8,128)(2,1)}, u32[]{:S(2)}, u32[]{:S(2)}) async-start(bf16[64,32,2048]{2,1,0:T(8,128)(2,1)} %bitcast.49), calls=%async_computation | async-start | bytes 16777216 | tf_op jit(solution)/shard_map/all_to_all | solution.py:63
  423.3 375.5 %all-to-all-start.1 = ((bf16[64,32,2048]{2,1,0:T(8,128)(2,1)}), bf16[64,32,2048]{2,1,0:T(8,128)(2,1)}, u32[]{:S(2)}, u32[]{:S(2)}) async-start(bf16[64,32,2048]{2,1,0:T(8,128)(2,1)} %bitcast.51), calls=%async_computation.1 | async-start | bytes 16777216 | tf_op jit(solution)/shard_map/all_to_all | solution.py:61
where the time goes:
time: 813 us; the launch traced here: 806 us
  waiting for transfers between devices  727 us (89%)
  matrix products  36.4 us (4%)
  starting transfers between devices  30.6 us (4%)
    all_to_all x1, waiting for transfers between devices, on_device(): lax.all_to_all(outgoing, 'expert', split_axis=0, concat_axis=0, tiled=True)  364 us
    all_to_all x1, waiting for transfers between devices, on_device(): lax.all_to_all(in_blocks(lax.all_to_all(outgoing, 'expert', split_axis=0,...  363 us
    dot_general x4, matrix products, expert_rows(): jnp.dot(hidden, down_part, preferred_element_type=jnp.float32)  21.3 us
    all_to_all x1, starting transfers between devices, on_device(): lax.all_to_all(outgoing, 'expert', split_axis=0, concat_axis=0, tiled=True)  18.5 us
  transfers between devices with their start and end apart: 2, of which 2 were waited for; matrix products, arithmetic and copies ran while one was open for 0% of the time, Pallas kernels for 0%

commit v1 on v0

v1 whole, which is shorter than its diff:
```python
import functools

import jax
import jax.numpy as jnp
from jax import lax
from jax.experimental import pallas as pl
from jax.experimental.pallas import tpu as pltpu
from jax.sharding import PartitionSpec as P

CAP = 32
Q = 16
HALF = 32
MESH = pl.DeviceIdType.MESH


def kernel(nz, tok, gate, up, down, ids, rw, out, tokbuf, rs, contrib, hid, gb, ub, wb, sht, shr, shc,
           ag_send, ag_recv, rs_send, rs_recv, own_sem, sib_send, sib_recv, x_send, x_recv, fw_send, fw_recv,
           sh_send, sh_recv):
    nh = nz // 2
    features = tok.shape[1]
    hdev = gate.shape[1]
    d = lax.axis_index("dp")
    e = lax.axis_index("expert")
    z = e // 4
    core = lax.rem(e, 2)
    x_lo = lax.rem(e // 2, 2)
    x_hi = lax.rem(d, 2)
    n_exp = 4 * nz
    zp = lax.rem(e + 4, n_exp)
    zm = lax.rem(e + n_exp - 4, n_exp)
    sib = e + 1 - 2 * core
    xq = e + 2 - 4 * x_lo
    d_other = d + 1 - 2 * x_hi

    def dev(dd, ee):
        return {"dp": dd, "expert": ee}

    barrier = pltpu.get_barrier_semaphore()
    peers = [(d, sib), (d, xq), (d_other, xq)] + [(d, lax.rem(e + 4 * k, n_exp)) for k in range(1, nz)]
    for dd, ee in peers:
        pl.semaphore_signal(barrier, inc=1, device_id=dev(dd, ee), device_id_type=MESH)
    pl.semaphore_wait(barrier, len(peers))

    def ag_has(dirn, t, q):
        return t < nh or (t == nh and q == dirn)

    def ag_copy(dirn, t, half, q):
        if dirn == 0:
            src_slot, dst_slot, target = t - 1, t, zp
        else:
            src_slot, dst_slot, target = (nz - t + 1) % nz, nz - t, zm
        if t == 1:
            src = tok.at[pl.ds(half * HALF + q * Q, Q), :]
        else:
            src = tokbuf.at[half, pl.ds(src_slot * HALF + q * Q, Q), :]
        i = half * 2 + q
        return pltpu.make_async_remote_copy(
            src_ref=src,
            dst_ref=tokbuf.at[half, pl.ds(dst_slot * HALF + q * Q, Q), :],
            send_sem=ag_send.at[dirn, t - 1, i],
            recv_sem=ag_recv.at[dirn, t - 1, i],
            device_id=dev(d, target),
            device_id_type=MESH,
        )

    def ag_first(half):
        for q in range(2):
            for dirn in range(2):
                if ag_has(dirn, 1, q):
                    ag_copy(dirn, 1, half, q).start()

    def rs_has(dirn, t, q):
        return t > 1 or q == 1 - dirn

    def rs_copy(dirn, t, half, q):
        if dirn == 0:
            src_slot, dst_slot, target = nh - 1 + t, nh + t, zp
        else:
            src_slot, dst_slot, target = nh + 1 - t, nh - t, zm
        i = half * 2 + q
        return pltpu.make_async_remote_copy(
            src_ref=rs.at[half, src_slot, pl.ds(q * Q, Q), :],
            dst_ref=rs.at[half, dst_slot, pl.ds(q * Q, Q), :],
            send_sem=rs_send.at[dirn, t - 1, i],
            recv_sem=rs_recv.at[dirn, t - 1, i],
            device_id=dev(d, target),
            device_id_type=MESH,
        )

    def rs_hop(dirn, t, half, q):
        if not rs_has(dirn, t, q):
            return
        slot = nh - 1 + t if dirn == 0 else nh + 1 - t
        rows = pl.ds(q * Q, Q)
        total = contrib[half, pl.ds(slot * HALF + q * Q, Q), :]
        if t > 1 and rs_has(dirn, t - 1, q):
            rs_copy(dirn, t - 1, half, q).wait_recv()
            total = total + rs[half, slot, rows, :].astype(jnp.float32)
        rs[half, slot, rows, :] = total.astype(jnp.bfloat16)
        rs_copy(dirn, t, half, q).start()

    def rs_last(half, q):
        rows = pl.ds(q * Q, Q)
        rs_copy(0, nh, half, q).wait_recv()
        rs_copy(1, nh, half, q).wait_recv()
        total = contrib[half, pl.ds(q * Q, Q), :]
        total = total + rs[half, 0, rows, :].astype(jnp.float32) + rs[half, nz, rows, :].astype(jnp.float32)
        out[pl.ds(half * HALF + q * Q, Q), :] = total.astype(jnp.bfloat16)

    sources = (gate, up, down)

    def whole(i, role):
        if i == 2:
            return wb.at[pl.ds(role * hdev, hdev), :]
        return (gb, ub)[i].at[role]

    def part(i, role, side):
        if i == 2:
            return wb.at[pl.ds(role * hdev + side * (hdev // 2), hdev // 2), :]
        return (gb, ub)[i].at[role, pl.ds(side * (features // 2), features // 2), :]

    def own_copy(i):
        return pltpu.make_async_copy(sources[i], whole(i, 0), own_sem.at[i])

    def sib_copy(i):
        return pltpu.make_async_remote_copy(
            src_ref=sources[i], dst_ref=whole(i, 1), send_sem=sib_send.at[i], recv_sem=sib_recv.at[i],
            device_id=dev(d, sib), device_id_type=MESH)

    def x_copy(i, side):
        size = sources[i].shape[0] // 2
        return pltpu.make_async_remote_copy(
            src_ref=sources[i].at[pl.ds(side * size, size), :], dst_ref=part(i, 2, side),
            send_sem=x_send.at[i, side], recv_sem=x_recv.at[i, side],
            device_id=dev(d if side == 0 else d_other, xq), device_id_type=MESH)

    def fw_copy(i, side):
        return pltpu.make_async_remote_copy(
            src_ref=part(i, 2, side), dst_ref=part(i, 3, side),
            send_sem=fw_send.at[i, side], recv_sem=fw_recv.at[i, side],
            device_id=dev(d, sib), device_id_type=MESH)

    def forward(i):
        for side in range(2):
            x_copy(i, side).wait_recv()
            fw_copy(i, side).start()

    def arrive(i, role):
        if role == 0:
            own_copy(i).wait()
        elif role == 1:
            sib_copy(i).wait_recv()
        elif role == 3:
            for side in range(2):
                fw_copy(i, side).wait_recv()

    def share_copy(k):
        there = lax.rem(z + k, nz)
        return pltpu.make_async_remote_copy(
            src_ref=sht.at[there], dst_ref=shr.at[k], send_sem=sh_send.at[k], recv_sem=sh_recv.at[k],
            device_id=dev(d, lax.rem(e + 4 * k, n_exp)), device_id_type=MESH)

    def make_shares():
        lane = lax.broadcasted_iota(jnp.int32, (64, 128), 1)
        counts = jnp.zeros((64, 128), jnp.float32)
        raw = jnp.zeros((64, 128), jnp.float32)
        for k in range(ids.shape[1]):
            match = ids[:, k:k + 1] == lane
            counts = counts + jnp.where(match, 1.0, 0.0)
            raw = raw + jnp.where(match, rw[:, k:k + 1], 0.0)
        before = lax.broadcasted_iota(jnp.int32, (64, 64), 1) < lax.broadcasted_iota(jnp.int32, (64, 64), 0)
        places = jnp.dot(jnp.where(before, 1.0, 0.0).astype(jnp.bfloat16), counts.astype(jnp.bfloat16),
                         preferred_element_type=jnp.float32)
        shares = jnp.where((counts == 1.0) & (places < CAP), raw, 0.0)
        turned = jnp.concatenate([shares, jnp.zeros((64, 128), jnp.float32)], axis=0).T
        for i in range(nz):
            sht[i, :, :] = turned[i:i + 1, :]
        for k in range(1, nz):
            share_copy(k).start()

    def take_shares():
        diag = lax.broadcasted_iota(jnp.int32, (64, 128), 1) == lax.broadcasted_iota(jnp.int32, (64, 128), 0)
        for k in range(nz):
            if k == 0:
                row = sht[z]
            else:
                share_copy(k).wait_recv()
                row = shr[k]
            column = jnp.sum(jnp.where(diag, row, 0.0), axis=1, keepdims=True)
            shc[0, pl.ds(k * HALF, HALF), :] = column[:HALF]
            shc[1, pl.ds(k * HALF, HALF), :] = column[HALF:]

    def hidden(half, role):
        tile = min(256, nz * HALF)

        def body(m, carry):
            rows = pl.ds(pl.multiple_of(m * tile, tile), tile)
            x = tokbuf[half, rows, :]
            g = jnp.dot(x, gb[role], preferred_element_type=jnp.float32)
            v = jnp.dot(x, ub[role], preferred_element_type=jnp.float32)
            hid[rows, role * hdev:(role + 1) * hdev] = (g / (1.0 + jnp.exp(-g)) * v).astype(jnp.bfloat16)
            return carry

        lax.fori_loop(0, nz * HALF // tile, body, 0)

    def project(half, n):
        tile = min(256, nz * HALF)
        width = features // 4

        def body(m, carry):
            rows = pl.ds(pl.multiple_of(m * tile, tile), tile)
            cols = slice(n * width, (n + 1) * width)
            acc = jnp.dot(hid[rows, :], wb[:, cols], preferred_element_type=jnp.float32)
            contrib[half, rows, cols] = acc * shc[half, rows, :]
            return carry

        lax.fori_loop(0, nz * HALF // tile, body, 0)

    ag_first(0)
    for i in range(3):
        for side in range(2):
            x_copy(i, side).start()
    for i in range(3):
        sib_copy(i).start()
        own_copy(i).start()
    for half in range(2):
        pltpu.make_async_copy(tok.at[pl.ds(half * HALF, HALF), :], tokbuf.at[half, pl.ds(0, HALF), :],
                              own_sem.at[3 + half]).start()
    make_shares()

    def spread(half, t):
        for q in range(2):
            for dirn in range(2):
                if ag_has(dirn, t, q):
                    ag_copy(dirn, t, half, q).wait_recv()
                if t < nh and ag_has(dirn, t + 1, q):
                    ag_copy(dirn, t + 1, half, q).start()

    for t in range(1, nh + 1):
        spread(0, t)
        if t == max(1, nh - 2):
            ag_first(1)
        if t == max(1, nh - 2):
            forward(0)
    for half in range(2):
        pltpu.make_async_copy(tok.at[pl.ds(half * HALF, HALF), :], tokbuf.at[half, pl.ds(0, HALF), :],
                              own_sem.at[3 + half]).wait()

    def work(half, t):
        step = (t - 1) * 8 // nh
        steps = max(1, 8 // nh)
        for s in range(step, step + steps):
            if s < 4:
                if half == 0:
                    arrive(0, s)
                    arrive(1, s)
                hidden(half, s)
            else:
                if half == 0 and s == 4:
                    take_shares()
                    forward(2)
                    for role in range(4):
                        arrive(2, role)
                project(half, s - 4)
            if half == 0 and s == 1:
                forward(1)

    for t in range(1, nh + 1):
        spread(1, t)
        work(0, t)

    for t in range(1, nh + 1):
        for q in range(2):
            for dirn in range(2):
                rs_hop(dirn, t, 0, q)
        work(1, t)
    for t in range(1, nh + 1):
        for q in range(2):
            for dirn in range(2):
                rs_hop(dirn, t, 1, q)
        if t == 2:
            rs_last(0, 0)
            rs_last(0, 1)
        if t == 3:
            for half in range(2):
                for tt in range(1, nh + 1):
                    for q in range(2):
                        for dirn in range(2):
                            if ag_has(dirn, tt, q):
                                ag_copy(dirn, tt, half, q).wait_send()
        if t == 4:
            for i in range(3):
                sib_copy(i).wait_send()
                for side in range(2):
                    x_copy(i, side).wait_send()
                    fw_copy(i, side).wait_send()
            for k in range(1, nz):
                share_copy(k).wait_send()
    for q in range(2):
        rs_last(1, q)
    for half in range(2):
        for t in range(1, nh + 1):
            for q in range(2):
                for dirn in range(2):
                    if rs_has(dirn, t, q):
                        rs_copy(dirn, t, half, q).wait_send()


def solution(mesh):
    nz = mesh.shape["expert"] // 4
    nh = nz // 2

    def on_device(tokens, gate, up, down, ids, rw):
        rows, features = tokens.shape
        hdev = gate.shape[1]
        dma = pltpu.SemaphoreType.DMA
        flops = 2 * rows * nz * features * 4 * hdev * 3
        return pl.pallas_call(
            functools.partial(kernel, nz),
            out_shape=jax.ShapeDtypeStruct((rows, features), jnp.bfloat16),
            in_specs=[pl.BlockSpec(memory_space=pl.ANY)] * 4 + [pl.BlockSpec(memory_space=pltpu.VMEM)] * 2,
            out_specs=pl.BlockSpec(memory_space=pltpu.VMEM),
            scratch_shapes=[
                pltpu.VMEM((2, nz * HALF, features), jnp.bfloat16),
                pltpu.VMEM((2, nz + 1, HALF, features), jnp.bfloat16),
                pltpu.VMEM((2, nz * HALF, features), jnp.float32),
                pltpu.VMEM((nz * HALF, 4 * hdev), jnp.bfloat16),
                pltpu.VMEM((4, features, hdev), jnp.bfloat16),
                pltpu.VMEM((4, features, hdev), jnp.bfloat16),
                pltpu.VMEM((4 * hdev, features), jnp.bfloat16),
                pltpu.VMEM((nz, 1, 128), jnp.float32),
                pltpu.VMEM((nz, 1, 128), jnp.float32),
                pltpu.VMEM((2, nz * HALF, 1), jnp.float32),
                dma((2, nh, 4)),
                dma((2, nh, 4)),
                dma((2, nh, 4)),
                dma((2, nh, 4)),
                dma((5,)),
                dma((3,)),
                dma((3,)),
                dma((3, 2)),
                dma((3, 2)),
                dma((3, 2)),
                dma((3, 2)),
                dma((nz,)),
                dma((nz,)),
            ],
            compiler_params=pltpu.CompilerParams(
                collective_id=0, has_side_effects=True, vmem_limit_bytes=56 * 1024 * 1024
            ),
            cost_estimate=pl.CostEstimate(flops=flops, bytes_accessed=4 * 1024 * 1024, transcendentals=0),
        )(tokens, gate, up, down, ids, rw)

    return jax.shard_map(
        on_device,
        mesh=mesh,
        in_specs=(
            P(("dp", "expert"), None),
            P(None, "expert"),
            P(None, "expert"),
            P("expert", None),
            P(("dp", "expert"), None),
            P(("dp", "expert"), None),
        ),
        out_specs=P(("dp", "expert"), None),
        check_vma=False,
    )
```

time: 813 us -> 145 us (0.18)
  the two profiles are of different devices: /device:TPU:1 before, /device:TPU:12 now
where the time goes in v1:
time: 145 us
  Pallas kernels  141 us (97%)
  local copies, waits for them, and re-layouts  3.76 us (3%)
    pallas_call x1, Pallas kernels, on_device(): pl.pallas_call(functools.partial(kernel, nz), out_shape=jax.ShapeDtypeStr...  141 us
    unnamed x5, local copies, waits for them, and re-layouts  3.76 us

profile of v1, /device:TPU:12, one launch (start us, length us, event | category | flops | bytes accessed | tf_op | source)
XLA Modules:
  0.0 145.2 jit_solution(10309067008384292728)
XLA Ops:
  0.0 0.0 copy-start
  0.0 1.4 copy.7.ids
  1.4 0.0 copy-done
  1.4 0.7 copy.8.rw
  2.1 141.4 %shard_map.64 = bf16[64,2048]{1,0:T(8,128)(2,1)} custom-call(bf16[64,2048]{1,0:T(8,128)(2,1)} %tok.1, bf16[2048,256]{1,0:T(8,128)(2,1)} %gate.1, bf16[2048,256]{1,0:T(8,128)(2,1)} %up.1, bf16[256,2048]{1,0:T(8,128)(2,1)} %down.1, s32[64,8]{1,0:T(8,128)} %copy.7.ids, f32[64,8]{1,0:T(8,128)} %copy.8.rw), custom_call_target="tpu_custom_call" | custom-call | flops 12884901888 | bytes 4194304 | tf_op jit(solution)/shard_map/pallas_call | solution.py:318
  143.5 1.7 %copy.10 = bf16[64,2048]{1,0:T(8,128)(2,1)} copy(bf16[64,2048]{1,0:T(8,128)(2,1)} %shard_map.64) | data formatting | bytes 524288
Async XLA Ops:
  0.0 1.4 copy-start

commit v2 on v1

--- a/solution.py
+++ b/solution.py
@@ -13,10 +13,12 @@
 MESH = pl.DeviceIdType.MESH
 
 
-def kernel(nz, tok, gate, up, down, ids, rw, out, tokbuf, rs, contrib, hid, gb, ub, wb, sht, shr, shc,
+def kernel(nz, tok, gate, up, down, ids, rw, out, tokbuf, rs, contrib, hid, gb, ub, wb, shr, shc,
            ag_send, ag_recv, rs_send, rs_recv, own_sem, sib_send, sib_recv, x_send, x_recv, fw_send, fw_recv,
            sh_send, sh_recv):
     nh = nz // 2
+    order = [0] + [s for t in range(1, nh) for s in (t, nz - t)] + [nh]
+    place = {slot: i * HALF for i, slot in enumerate(order)}
     features = tok.shape[1]
     hdev = gate.shape[1]
     d = lax.axis_index("dp")
@@ -36,10 +38,9 @@
         return {"dp": dd, "expert": ee}
 
     barrier = pltpu.get_barrier_semaphore()
-    peers = [(d, sib), (d, xq), (d_other, xq)] + [(d, lax.rem(e + 4 * k, n_exp)) for k in range(1, nz)]
+    peers = [(d, zp), (d, zm), (d, xq), (d_other, xq), (d, sib)]
     for dd, ee in peers:
         pl.semaphore_signal(barrier, inc=1, device_id=dev(dd, ee), device_id_type=MESH)
-    pl.semaphore_wait(barrier, len(peers))
 
     def ag_has(dirn, t, q):
         return t < nh or (t == nh and q == dirn)
@@ -52,11 +53,11 @@
         if t == 1:
             src = tok.at[pl.ds(half * HALF + q * Q, Q), :]
         else:
-            src = tokbuf.at[half, pl.ds(src_slot * HALF + q * Q, Q), :]
+            src = tokbuf.at[half, pl.ds(place[src_slot] + q * Q, Q), :]
         i = half * 2 + q
         return pltpu.make_async_remote_copy(
             src_ref=src,
-            dst_ref=tokbuf.at[half, pl.ds(dst_slot * HALF + q * Q, Q), :],
+            dst_ref=tokbuf.at[half, pl.ds(place[dst_slot] + q * Q, Q), :],
             send_sem=ag_send.at[dirn, t - 1, i],
             recv_sem=ag_recv.at[dirn, t - 1, i],
             device_id=dev(d, target),
@@ -92,7 +93,7 @@
             return
         slot = nh - 1 + t if dirn == 0 else nh + 1 - t
         rows = pl.ds(q * Q, Q)
-        total = contrib[half, pl.ds(slot * HALF + q * Q, Q), :]
+        total = contrib[half, pl.ds(place[slot] + q * Q, Q), :]
         if t > 1 and rs_has(dirn, t - 1, q):
             rs_copy(dirn, t - 1, half, q).wait_recv()
             total = total + rs[half, slot, rows, :].astype(jnp.float32)
@@ -154,79 +155,77 @@
             for side in range(2):
                 fw_copy(i, side).wait_recv()
 
-    def share_copy(k):
-        there = lax.rem(z + k, nz)
-        return pltpu.make_async_remote_copy(
-            src_ref=sht.at[there], dst_ref=shr.at[k], send_sem=sh_send.at[k], recv_sem=sh_recv.at[k],
-            device_id=dev(d, lax.rem(e + 4 * k, n_exp)), device_id_type=MESH)
+    def share_has(dirn, t):
+        return t < nh or dirn == 0
+
+    def share_copy(dirn, t):
+        if dirn == 0:
+            src_slot, dst_slot, target = t - 1, t, zp
+        else:
+            src_slot, dst_slot, target = (nz - t + 1) % nz, nz - t, zm
+        return pltpu.make_async_remote_copy(
+            src_ref=shr.at[src_slot], dst_ref=shr.at[dst_slot],
+            send_sem=sh_send.at[dirn, t - 1], recv_sem=sh_recv.at[dirn, t - 1],
+            device_id=dev(d, target), device_id_type=MESH)
 
     def make_shares():
-        lane = lax.broadcasted_iota(jnp.int32, (64, 128), 1)
-        counts = jnp.zeros((64, 128), jnp.float32)
-        raw = jnp.zeros((64, 128), jnp.float32)
-        for k in range(ids.shape[1]):
-            match = ids[:, k:k + 1] == lane
+        experts = lax.broadcasted_iota(jnp.int32, (nz, 64), 0)
+        counts = jnp.zeros((nz, 64), jnp.float32)
+        raw = jnp.zeros((nz, 64), jnp.float32)
+        for k in range(ids.shape[0]):
+            match = ids[k:k + 1, :] == experts
             counts = counts + jnp.where(match, 1.0, 0.0)
-            raw = raw + jnp.where(match, rw[:, k:k + 1], 0.0)
-        before = lax.broadcasted_iota(jnp.int32, (64, 64), 1) < lax.broadcasted_iota(jnp.int32, (64, 64), 0)
-        places = jnp.dot(jnp.where(before, 1.0, 0.0).astype(jnp.bfloat16), counts.astype(jnp.bfloat16),
+            raw = raw + jnp.where(match, rw[k:k + 1, :], 0.0)
+        before = lax.broadcasted_iota(jnp.int32, (64, 64), 0) < lax.broadcasted_iota(jnp.int32, (64, 64), 1)
+        places = jnp.dot(counts.astype(jnp.bfloat16), jnp.where(before, 1.0, 0.0).astype(jnp.bfloat16),
                          preferred_element_type=jnp.float32)
         shares = jnp.where((counts == 1.0) & (places < CAP), raw, 0.0)
-        turned = jnp.concatenate([shares, jnp.zeros((64, 128), jnp.float32)], axis=0).T
-        for i in range(nz):
-            sht[i, :, :] = turned[i:i + 1, :]
-        for k in range(1, nz):
-            share_copy(k).start()
-
-    def take_shares():
-        diag = lax.broadcasted_iota(jnp.int32, (64, 128), 1) == lax.broadcasted_iota(jnp.int32, (64, 128), 0)
-        for k in range(nz):
-            if k == 0:
-                row = sht[z]
-            else:
-                share_copy(k).wait_recv()
-                row = shr[k]
-            column = jnp.sum(jnp.where(diag, row, 0.0), axis=1, keepdims=True)
-            shc[0, pl.ds(k * HALF, HALF), :] = column[:HALF]
-            shc[1, pl.ds(k * HALF, HALF), :] = column[HALF:]
-
-    def hidden(half, role):
-        tile = min(256, nz * HALF)
-
-        def body(m, carry):
-            rows = pl.ds(pl.multiple_of(m * tile, tile), tile)
-            x = tokbuf[half, rows, :]
-            g = jnp.dot(x, gb[role], preferred_element_type=jnp.float32)
-            v = jnp.dot(x, ub[role], preferred_element_type=jnp.float32)
-            hid[rows, role * hdev:(role + 1) * hdev] = (g / (1.0 + jnp.exp(-g)) * v).astype(jnp.bfloat16)
-            return carry
-
-        lax.fori_loop(0, nz * HALF // tile, body, 0)
-
-    def project(half, n):
-        tile = min(256, nz * HALF)
+        for k in range(nz // 8):
+            shr[0, :, k * 64:(k + 1) * 64] = shares[k * 8:(k + 1) * 8, :]
+
+    def take_shares(slots):
+        lane = lax.broadcasted_iota(jnp.int32, (64, 128), 1)
+        row = lax.broadcasted_iota(jnp.int32, (64, 128), 0)
+        diag = lane == row + 64 * (z // 8)
+        for slot in slots:
+            mine = shr[slot, pl.ds(lax.rem(z, 8), 1), :]
+            column = jnp.sum(jnp.where(diag, mine, 0.0), axis=1, keepdims=True)
+            shc[0, pl.ds(place[slot], HALF), :] = column[:HALF]
+            shc[1, pl.ds(place[slot], HALF), :] = column[HALF:]
+
+    tile = nz * HALF // 2
+
+    def hidden(half, m, role):
+        rows = pl.ds(m * tile, tile)
+        x = tokbuf[half, rows, :]
+        g = jnp.dot(x, gb[role], preferred_element_type=jnp.float32)
+        v = jnp.dot(x, ub[role], preferred_element_type=jnp.float32)
+        hid[half, rows, role * hdev:(role + 1) * hdev] = (g / (1.0 + jnp.exp(-g)) * v).astype(jnp.bfloat16)
+
+    def project(half, m, n):
+        rows = pl.ds(m * tile, tile)
         width = features // 4
-
-        def body(m, carry):
-            rows = pl.ds(pl.multiple_of(m * tile, tile), tile)
-            cols = slice(n * width, (n + 1) * width)
-            acc = jnp.dot(hid[rows, :], wb[:, cols], preferred_element_type=jnp.float32)
-            contrib[half, rows, cols] = acc * shc[half, rows, :]
-            return carry
-
-        lax.fori_loop(0, nz * HALF // tile, body, 0)
-
-    ag_first(0)
+        cols = slice(n * width, (n + 1) * width)
+        acc = jnp.dot(hid[half, rows, :], wb[:, cols], preferred_element_type=jnp.float32)
+        contrib[half, rows, cols] = acc * shc[half, rows, :]
+
     for i in range(3):
-        for side in range(2):
-            x_copy(i, side).start()
-    for i in range(3):
-        sib_copy(i).start()
         own_copy(i).start()
     for half in range(2):
         pltpu.make_async_copy(tok.at[pl.ds(half * HALF, HALF), :], tokbuf.at[half, pl.ds(0, HALF), :],
                               own_sem.at[3 + half]).start()
     make_shares()
+    pl.semaphore_wait(barrier, len(peers))
+
+    ag_first(0)
+    for dirn in range(2):
+        share_copy(dirn, 1).start()
+    ag_first(1)
+    for i in range(2):
+        for side in range(2):
+            x_copy(i, side).start()
+    for i in range(3):
+        sib_copy(i).start()
 
     def spread(half, t):
         for q in range(2):
@@ -236,51 +235,73 @@
                 if t < nh and ag_has(dirn, t + 1, q):
                     ag_copy(dirn, t + 1, half, q).start()
 
+    def spread_shares(t):
+        for dirn in range(2):
+            if share_has(dirn, t):
+                share_copy(dirn, t).wait_recv()
+            if t < nh and share_has(dirn, t + 1):
+                share_copy(dirn, t + 1).start()
+
     for t in range(1, nh + 1):
         spread(0, t)
-        if t == max(1, nh - 2):
-            ag_first(1)
-        if t == max(1, nh - 2):
+        spread_shares(t)
+        if t < nh:
+            spread(1, t)
+        if t == 2:
+            for side in range(2):
+                x_copy(2, side).start()
+        if t == 4:
+            for half in range(2):
+                pltpu.make_async_copy(tok.at[pl.ds(half * HALF, HALF), :], tokbuf.at[half, pl.ds(0, HALF), :],
+                                      own_sem.at[3 + half]).wait()
+            for role in range(2):
+                arrive(0, role)
+                arrive(1, role)
+                for half in range(2):
+                    hidden(half, 0, role)
+        if t == 5:
             forward(0)
-    for half in range(2):
-        pltpu.make_async_copy(tok.at[pl.ds(half * HALF, HALF), :], tokbuf.at[half, pl.ds(0, HALF), :],
-                              own_sem.at[3 + half]).wait()
-
-    def work(half, t):
-        step = (t - 1) * 8 // nh
-        steps = max(1, 8 // nh)
-        for s in range(step, step + steps):
-            if s < 4:
-                if half == 0:
-                    arrive(0, s)
-                    arrive(1, s)
-                hidden(half, s)
-            else:
-                if half == 0 and s == 4:
-                    take_shares()
-                    forward(2)
-                    for role in range(4):
-                        arrive(2, role)
-                project(half, s - 4)
-            if half == 0 and s == 1:
-                forward(1)
-
-    for t in range(1, nh + 1):
-        spread(1, t)
-        work(0, t)
-
-    for t in range(1, nh + 1):
+            forward(1)
+            for half in range(2):
+                hidden(half, 0, 2)
+        if t == 6:
+            arrive(0, 3)
+            arrive(1, 3)
+            for half in range(2):
+                hidden(half, 0, 3)
+            take_shares(order[:nz // 2])
+        if t == 7:
+            forward(2)
+            for role in range(4):
+                arrive(2, role)
+            for half in range(2):
+                for n in range(4):
+                    project(half, 0, n)
+
+    def last_tile(half):
+        for role in range(4):
+            hidden(half, 1, role)
+        if half == 0:
+            take_shares(order[nz // 2:])
+        for n in range(4):
+            project(half, 1, n)
+
+    def back(half, t):
         for q in range(2):
             for dirn in range(2):
-                rs_hop(dirn, t, 0, q)
-        work(1, t)
-    for t in range(1, nh + 1):
-        for q in range(2):
-            for dirn in range(2):
-                rs_hop(dirn, t, 1, q)
-        if t == 2:
-            rs_last(0, 0)
-            rs_last(0, 1)
+                if t == 1 or rs_has(dirn, 1, q):
+                    rs_hop(dirn, t if rs_has(dirn, t, q) else t + 1, half, q)
+                elif t > 2:
+                    rs_hop(dirn, t, half, q)
+
+    last_tile(0)
+    back(0, 1)
+    spread(1, nh)
+    last_tile(1)
+    back(1, 1)
+    for t in range(2, nh + 1):
+        for half in range(2):
+            back(half, t)
         if t == 3:
             for half in range(2):
                 for tt in range(1, nh + 1):
@@ -294,10 +315,13 @@
                 for side in range(2):
                     x_copy(i, side).wait_send()
                     fw_copy(i, side).wait_send()
-            for k in range(1, nz):
-                share_copy(k).wait_send()
-    for q in range(2):
-        rs_last(1, q)
+            for tt in range(1, nh + 1):
+                for dirn in range(2):
+                    if share_has(dirn, tt):
+                        share_copy(dirn, tt).wait_send()
+    for half in range(2):
+        for q in range(2):
+            rs_last(half, q)
     for half in range(2):
         for t in range(1, nh + 1):
             for q in range(2):
@@ -324,12 +348,11 @@
                 pltpu.VMEM((2, nz * HALF, features), jnp.bfloat16),
                 pltpu.VMEM((2, nz + 1, HALF, features), jnp.bfloat16),
                 pltpu.VMEM((2, nz * HALF, features), jnp.float32),
-                pltpu.VMEM((nz * HALF, 4 * hdev), jnp.bfloat16),
+                pltpu.VMEM((2, nz * HALF, 4 * hdev), jnp.bfloat16),
                 pltpu.VMEM((4, features, hdev), jnp.bfloat16),
                 pltpu.VMEM((4, features, hdev), jnp.bfloat16),
                 pltpu.VMEM((4 * hdev, features), jnp.bfloat16),
-                pltpu.VMEM((nz, 1, 128), jnp.float32),
-                pltpu.VMEM((nz, 1, 128), jnp.float32),
+                pltpu.VMEM((nz, 8, 128), jnp.float32),
                 pltpu.VMEM((2, nz * HALF, 1), jnp.float32),
                 dma((2, nh, 4)),
                 dma((2, nh, 4)),
@@ -342,14 +365,14 @@
                 dma((3, 2)),
                 dma((3, 2)),
                 dma((3, 2)),
-                dma((nz,)),
-                dma((nz,)),
+                dma((2, nh)),
+                dma((2, nh)),
             ],
             compiler_params=pltpu.CompilerParams(
                 collective_id=0, has_side_effects=True, vmem_limit_bytes=56 * 1024 * 1024
             ),
             cost_estimate=pl.CostEstimate(flops=flops, bytes_accessed=4 * 1024 * 1024, transcendentals=0),
-        )(tokens, gate, up, down, ids, rw)
+        )(tokens, gate, up, down, ids.T, rw.T)
 
     return jax.shard_map(
         on_device,

time: 145 us -> 113 us (0.78)
  the two profiles are of different devices: /device:TPU:12 before, /device:TPU:1 now
where the time goes in v2:
time: 113 us
  Pallas kernels  111 us (98%)
  local copies, waits for them, and re-layouts  1.67 us (1%)
    pallas_call x1, Pallas kernels, on_device(): pl.pallas_call(functools.partial(kernel, nz), out_shape=jax.ShapeDtypeStr...  111 us

profile of v2, /device:TPU:1, one launch (start us, length us, event | category | flops | bytes accessed | tf_op | source)
XLA Modules:
  0.0 113.0 jit_solution(6580868655768108875)
XLA Ops:
  0.0 111.3 %shard_map.64 = bf16[64,2048]{1,0:T(8,128)(2,1)} custom-call(bf16[64,2048]{1,0:T(8,128)(2,1)} %tok.1, bf16[2048,256]{1,0:T(8,128)(2,1)} %gate.1, bf16[2048,256]{1,0:T(8,128)(2,1)} %up.1, bf16[256,2048]{1,0:T(8,128)(2,1)} %down.1, s32[8,64]{1,0:T(8,128)} %bitcast.2, f32[8,64]{1,0:T(8,128)} %bitcast.3), custom_call_target="tpu_custom_call" | custom-call | flops 12884901888 | bytes 4194304 | tf_op jit(solution)/shard_map/pallas_call | solution.py:342
  111.3 1.7 %copy.8 = bf16[64,2048]{1,0:T(8,128)(2,1)} copy(bf16[64,2048]{1,0:T(8,128)(2,1)} %shard_map.64) | data formatting | bytes 524288

commit v3 on v2

v3 whole, which is shorter than its diff:
```python
import functools

import jax
import jax.numpy as jnp
from jax import lax
from jax.experimental import pallas as pl
from jax.experimental.pallas import tpu as pltpu
from jax.sharding import PartitionSpec as P

CAP = 32
Q = 16
HALF = 32
MESH = pl.DeviceIdType.MESH


def kernel(nz, tok, gate, up, down, ids_hbm, rw_hbm, out, tokbuf, rs, contrib, hid, gb, ub, wb, shr, shc, ids, rw, outbuf,
           ag_send, ag_recv, rs_send, rs_recv, own_sem, sib_send, sib_recv, x_send, x_recv, fw_send, fw_recv,
           sh_send, sh_recv, in_sem, out_sem):
    nh = nz // 2
    order = [0] + [s for t in range(1, nh) for s in (t, nz - t)] + [nh]
    early, middle, late, last = order[:nh], order[nh:nh + nh // 2], order[nh + nh // 2:-1], order[-1:]
    place, tiles, row = {}, {}, 0
    for name, slots, halves in (("A0", early, (0,)), ("A1", early, (1,)), ("B", middle, (0, 1)), ("C", late, (0, 1)), ("D", last, (0, 1))):
        tiles[name] = (row, len(slots) * len(halves) * HALF)
        for half in halves:
            for slot in slots:
                place[half, slot] = row
                row += HALF
    features = tok.shape[1]
    hdev = gate.shape[1]
    d = lax.axis_index("dp")
    e = lax.axis_index("expert")
    z = e // 4
    core = lax.rem(e, 2)
    x_lo = lax.rem(e // 2, 2)
    x_hi = lax.rem(d, 2)
    n_exp = 4 * nz
    zp = lax.rem(e + 4, n_exp)
    zm = lax.rem(e + n_exp - 4, n_exp)
    sib = e + 1 - 2 * core
    xq = e + 2 - 4 * x_lo
    d_other = d + 1 - 2 * x_hi

    def dev(dd, ee):
        return {"dp": dd, "expert": ee}

    barrier = pltpu.get_barrier_semaphore()
    peers = [(d, zp), (d, zm), (d, xq), (d_other, xq), (d, sib)]
    for dd, ee in peers:
        pl.semaphore_signal(barrier, inc=1, device_id=dev(dd, ee), device_id_type=MESH)

    def ag_has(dirn, t, q):
        return t < nh or (t == nh and q == dirn)

    def ag_copy(dirn, t, half, q):
        if dirn == 0:
            src_slot, dst_slot, target = t - 1, t, zp
        else:
            src_slot, dst_slot, target = (nz - t + 1) % nz, nz - t, zm
        if t == 1:
            src = tok.at[pl.ds(half * HALF + q * Q, Q), :]
        else:
            src = tokbuf.at[pl.ds(place[half, src_slot] + q * Q, Q), :]
        i = half * 2 + q
        return pltpu.make_async_remote_copy(
            src_ref=src,
            dst_ref=tokbuf.at[pl.ds(place[half, dst_slot] + q * Q, Q), :],
            send_sem=ag_send.at[dirn, t - 1, i],
            recv_sem=ag_recv.at[dirn, t - 1, i],
            device_id=dev(d, target),
            device_id_type=MESH,
        )

    def ag_first(half):
        for q in range(2):
            for dirn in range(2):
                if ag_has(dirn, 1, q):
                    ag_copy(dirn, 1, half, q).start()

    def rs_has(dirn, t, q):
        return t > 1 or q == 1 - dirn

    def rs_copy(dirn, t, half, q):
        if dirn == 0:
            src_slot, dst_slot, target = nh - 1 + t, nh + t, zp
        else:
            src_slot, dst_slot, target = nh + 1 - t, nh - t, zm
        i = half * 2 + q
        return pltpu.make_async_remote_copy(
            src_ref=rs.at[half, src_slot, pl.ds(q * Q, Q), :],
            dst_ref=rs.at[half, dst_slot, pl.ds(q * Q, Q), :],
            send_sem=rs_send.at[dirn, t - 1, i],
            recv_sem=rs_recv.at[dirn, t - 1, i],
            device_id=dev(d, target),
            device_id_type=MESH,
        )

    def rs_hop(dirn, t, half, q):
        if not rs_has(dirn, t, q):
            return
        slot = nh - 1 + t if dirn == 0 else nh + 1 - t
        rows = pl.ds(q * Q, Q)
        total = contrib[pl.ds(place[half, slot] + q * Q, Q), :]
        if t > 1 and rs_has(dirn, t - 1, q):
            rs_copy(dirn, t - 1, half, q).wait_recv()
            total = total + rs[half, slot, rows, :].astype(jnp.float32)
        rs[half, slot, rows, :] = total.astype(jnp.bfloat16)
        rs_copy(dirn, t, half, q).start()

    def rs_last(half, q):
        rows = pl.ds(q * Q, Q)
        rs_copy(0, nh, half, q).wait_recv()
        rs_copy(1, nh, half, q).wait_recv()
        total = contrib[pl.ds(place[half, 0] + q * Q, Q), :]
        total = total + rs[half, 0, rows, :].astype(jnp.float32) + rs[half, nz, rows, :].astype(jnp.float32)
        outbuf[pl.ds(half * HALF + q * Q, Q), :] = total.astype(jnp.bfloat16)
        out_copy(half, q).start()

    def out_copy(half, q):
        rows = pl.ds(half * HALF + q * Q, Q)
        return pltpu.make_async_copy(outbuf.at[rows, :], out.at[rows, :], out_sem.at[half * 2 + q])

    sources = (gate, up, down)

    def whole(i, role):
        if i == 2:
            return wb.at[pl.ds(role * hdev, hdev), :]
        return (gb, ub)[i].at[role]

    def part(i, role, side):
        if i == 2:
            return wb.at[pl.ds(role * hdev + side * (hdev // 2), hdev // 2), :]
        return (gb, ub)[i].at[role, pl.ds(side * (features // 2), features // 2), :]

    def own_copy(i):
        return pltpu.make_async_copy(sources[i], whole(i, 0), own_sem.at[i])

    def piece(i, role, k):
        size = sources[i].shape[0] // 4
        if i == 2:
            return wb.at[pl.ds(role * hdev + k * size, size), :]
        return (gb, ub)[i].at[role, pl.ds(k * size, size), :]

    def sib_copy(i, k):
        size = sources[i].shape[0] // 4
        return pltpu.make_async_remote_copy(
            src_ref=sources[i].at[pl.ds(k * size, size), :], dst_ref=piece(i, 1, k),
            send_sem=sib_send.at[i, k], recv_sem=sib_recv.at[i, k],
            device_id=dev(d, sib), device_id_type=MESH)

    def x_copy(i, side):
        size = sources[i].shape[0] // 2
        return pltpu.make_async_remote_copy(
            src_ref=sources[i].at[pl.ds(side * size, size), :], dst_ref=part(i, 2, side),
            send_sem=x_send.at[i, side], recv_sem=x_recv.at[i, side],
            device_id=dev(d if side == 0 else d_other, xq), device_id_type=MESH)

    def fw_copy(i, k):
        return pltpu.make_async_remote_copy(
            src_ref=piece(i, 2, k), dst_ref=piece(i, 3, k),
            send_sem=fw_send.at[i, k], recv_sem=fw_recv.at[i, k],
            device_id=dev(d, sib), device_id_type=MESH)

    def forward(i, side):
        x_copy(i, side).wait_recv()
        for k in range(2):
            fw_copy(i, side * 2 + k).start()

    def arrive(i, role):
        if role == 0:
            own_copy(i).wait()
        for k in range(4):
            if role == 1:
                sib_copy(i, k).wait_recv()
            elif role == 3:
                fw_copy(i, k).wait_recv()

    def share_has(dirn, t):
        return t < nh or dirn == 0

    def share_copy(dirn, t):
        if dirn == 0:
            src_slot, dst_slot, target = t - 1, t, zp
        else:
            src_slot, dst_slot, target = (nz - t + 1) % nz, nz - t, zm
        return pltpu.make_async_remote_copy(
            src_ref=shr.at[src_slot], dst_ref=shr.at[dst_slot],
            send_sem=sh_send.at[dirn, t - 1], recv_sem=sh_recv.at[dirn, t - 1],
            device_id=dev(d, target), device_id_type=MESH)

    def make_shares():
        experts = lax.broadcasted_iota(jnp.int32, (nz, 64), 0)
        counts = jnp.zeros((nz, 64), jnp.float32)
        raw = jnp.zeros((nz, 64), jnp.float32)
        for k in range(ids.shape[0]):
            match = ids[k:k + 1, :] == experts
            counts = counts + jnp.where(match, 1.0, 0.0)
            raw = raw + jnp.where(match, rw[k:k + 1, :], 0.0)
        before = lax.broadcasted_iota(jnp.int32, (64, 64), 0) < lax.broadcasted_iota(jnp.int32, (64, 64), 1)
        places = jnp.dot(counts.astype(jnp.bfloat16), jnp.where(before, 1.0, 0.0).astype(jnp.bfloat16),
                         preferred_element_type=jnp.float32)
        shares = jnp.where((counts == 1.0) & (places < CAP), raw, 0.0)
        for k in range(nz // 8):
            shr[0, :, k * 64:(k + 1) * 64] = shares[k * 8:(k + 1) * 8, :]

    def take_shares(slots):
        lane = lax.broadcasted_iota(jnp.int32, (64, 128), 1)
        row = lax.broadcasted_iota(jnp.int32, (64, 128), 0)
        diag = lane == row + 64 * (z // 8)
        for slot in slots:
            mine = shr[slot, pl.ds(lax.rem(z, 8), 1), :]
            column = jnp.sum(jnp.where(diag, mine, 0.0), axis=1, keepdims=True)
            for half in range(2):
                shc[pl.ds(place[half, slot], HALF), :] = column[half * HALF:(half + 1) * HALF]

    def hidden(m, role):
        rows = pl.ds(*tiles[m])
        x = tokbuf[rows, :]
        g = jnp.dot(x, gb[role], preferred_element_type=jnp.float32)
        v = jnp.dot(x, ub[role], preferred_element_type=jnp.float32)
        hid[rows, role * hdev:(role + 1) * hdev] = (g / (1.0 + jnp.exp(-g)) * v).astype(jnp.bfloat16)

    def project(m, n):
        rows = pl.ds(*tiles[m])
        width = features // 4
        cols = slice(n * width, (n + 1) * width)
        acc = jnp.dot(hid[rows, :], wb[:, cols], preferred_element_type=jnp.float32)
        contrib[rows, cols] = acc * shc[rows, :]

    own_tokens = [
        pltpu.make_async_copy(tok.at[pl.ds(half * HALF, HALF), :], tokbuf.at[pl.ds(place[half, 0], HALF), :], own_sem.at[3 + half])
        for half in range(2)
    ]
    small = [pltpu.make_async_copy(ids_hbm, ids, in_sem.at[0]), pltpu.make_async_copy(rw_hbm, rw, in_sem.at[1])]
    for copy in small:
        copy.start()
    for i in range(3):
        own_copy(i).start()
    for copy in own_tokens:
        copy.start()
    for copy in small:
        copy.wait()
    make_shares()
    pl.semaphore_wait(barrier, len(peers))

    ag_first(0)
    for dirn in range(2):
        share_copy(dirn, 1).start()
    ag_first(1)
    for i in range(2):
        for side in range(2):
            x_copy(i, side).start()

    def spread(half, t, q):
        for dirn in range(2):
            if ag_has(dirn, t, q):
                ag_copy(dirn, t, half, q).wait_recv()
            if t < nh and ag_has(dirn, t + 1, q):
                ag_copy(dirn, t + 1, half, q).start()

    def spread_shares(t):
        for dirn in range(2):
            if share_has(dirn, t):
                share_copy(dirn, t).wait_recv()
            if t < nh and share_has(dirn, t + 1):
                share_copy(dirn, t + 1).start()

    copies, products = [], []

    def step(hop):
        for queue in (copies, products):
            if queue and queue[0][0] <= hop:
                call = queue.pop(0)
                call[1](*call[2:])

    def arrive_both(role):
        arrive(0, role)
        arrive(1, role)

    def own_arrived():
        for copy in own_tokens:
            copy.wait()
        arrive_both(0)

    def start_sib(i, k):
        sib_copy(i, k).start()

    def start_down():
        for side in range(2):
            x_copy(2, side).start()

    def arrive_down():
        for role in range(4):
            arrive(2, role)

    for k in range(4):
        for i in range(2):
            copies.append((1, start_sib, i, k))
    copies.append((2, start_down))
    for k in range(4):
        copies.append((3, start_sib, 2, k))
    for i in range(2):
        for side in range(2):
            copies.append((4.2, forward, i, side))
    for side in range(2):
        copies.append((6.3, forward, 2, side))

    products.append((4, own_arrived))
    products.append((4.1, arrive_both, 1))
    for role in range(2):
        for half in range(2):
            products.append((4.1 + half * 0.2, hidden, ("A0", "A1")[half], role))
    for half in range(2):
        products.append((5.2, hidden, ("A0", "A1")[half], 2))
    products.append((6, arrive_both, 3))
    for half in range(2):
        products.append((6, hidden, ("A0", "A1")[half], 3))
    for role in range(4):
        products.append((6.3, hidden, "B", role))
    products.append((6.3, take_shares, order[:nh + nh // 2]))

    for t in range(1, nh):
        for half in range(2):
            for q in range(2):
                spread(half, t, q)
                if half == 0 and q == 1:
                    spread_shares(t)
                step(t + 0.1 * (2 * half + q))
    while copies or products:
        step(nh)

    for role in range(4):
        hidden("C", role)
    arrive_down()
    take_shares(late)
    for n in range(4):
        project("C", n)
    for half in range(2):
        rs_hop(0, 2, half, 0)
        rs_hop(1, 2, half, 1)
    for n in range(4):
        project("B", n)
    for half in range(2):
        for q in range(2):
            spread(half, nh, q)
    spread_shares(nh)
    for role in range(4):
        hidden("D", role)
    take_shares(last)
    for n in range(4):
        project("D", n)
    for half in range(2):
        rs_hop(0, 1, half, 1)
        rs_hop(1, 1, half, 0)

    def sent():
        for half in range(2):
            for tt in range(1, nh + 1):
                for q in range(2):
                    for dirn in range(2):
                        if ag_has(dirn, tt, q):
                            ag_copy(dirn, tt, half, q).wait_send()

    def weights_sent():
        for i in range(3):
            for k in range(4):
                sib_copy(i, k).wait_send()
                fw_copy(i, k).wait_send()
            for side in range(2):
                x_copy(i, side).wait_send()
        for tt in range(1, nh + 1):
            for dirn in range(2):
                if share_has(dirn, tt):
                    share_copy(dirn, tt).wait_send()

    for half in range(2):
        for n in range(4):
            products.append((2, project, ("A0", "A1")[half], n))
    products.append((5, sent))
    products.append((5, weights_sent))

    for t in range(2, nh + 1):
        for half in range(2):
            if t < nh:
                rs_hop(0, t + 1, half, 0)
                rs_hop(1, t + 1, half, 1)
            step(t)
            rs_hop(0, t, half, 1)
            rs_hop(1, t, half, 0)
            step(t)
    for half in range(2):
        for q in range(2):
            rs_last(half, q)
    for half in range(2):
        for t in range(1, nh + 1):
            for q in range(2):
                for dirn in range(2):
                    if rs_has(dirn, t, q):
                        rs_copy(dirn, t, half, q).wait_send()
    for half in range(2):
        for q in range(2):
            out_copy(half, q).wait()


def solution(mesh):
    nz = mesh.shape["expert"] // 4
    nh = nz // 2

    def on_device(tokens, gate, up, down, ids, rw):
        rows, features = tokens.shape
        hdev = gate.shape[1]
        dma = pltpu.SemaphoreType.DMA
        flops = 2 * rows * nz * features * 4 * hdev * 3
        return pl.pallas_call(
            functools.partial(kernel, nz),
            out_shape=jax.ShapeDtypeStruct((rows, features), jnp.bfloat16),
            in_specs=[pl.BlockSpec(memory_space=pl.ANY)] * 6,
            out_specs=pl.BlockSpec(memory_space=pl.ANY),
            scratch_shapes=[
                pltpu.VMEM((nz * rows, features), jnp.bfloat16),
                pltpu.VMEM((2, nz + 1, HALF, features), jnp.bfloat16),
                pltpu.VMEM((nz * rows, features), jnp.float32),
                pltpu.VMEM((nz * rows, 4 * hdev), jnp.bfloat16),
                pltpu.VMEM((4, features, hdev), jnp.bfloat16),
                pltpu.VMEM((4, features, hdev), jnp.bfloat16),
                pltpu.VMEM((4 * hdev, features), jnp.bfloat16),
                pltpu.VMEM((nz, 8, 128), jnp.float32),
                pltpu.VMEM((nz * rows, 1), jnp.float32),
                pltpu.VMEM((ids.shape[1], rows), jnp.int32),
                pltpu.VMEM((ids.shape[1], rows), jnp.float32),
                pltpu.VMEM((rows, features), jnp.bfloat16),
                dma((2, nh, 4)),
                dma((2, nh, 4)),
                dma((2, nh, 4)),
                dma((2, nh, 4)),
                dma((5,)),
                dma((3, 4)),
                dma((3, 4)),
                dma((3, 2)),
                dma((3, 2)),
                dma((3, 4)),
                dma((3, 4)),
                dma((2, nh)),
                dma((2, nh)),
                dma((2,)),
                dma((4,)),
            ],
            compiler_params=pltpu.CompilerParams(
                collective_id=0, has_side_effects=True, vmem_limit_bytes=56 * 1024 * 1024
            ),
            cost_estimate=pl.CostEstimate(flops=flops, bytes_accessed=4 * 1024 * 1024, transcendentals=0),
        )(tokens, gate, up, down, ids.T, rw.T)

    return jax.shard_map(
        on_device,
        mesh=mesh,
        in_specs=(
            P(("dp", "expert"), None),
            P(None, "expert"),
            P(None, "expert"),
            P("expert", None),
            P(("dp", "expert"), None),
            P(("dp", "expert"), None),
        ),
        out_specs=P(("dp", "expert"), None),
        check_vma=False,
    )
```

time: 113 us -> 108 us (0.956)
  the two profiles are of different devices: /device:TPU:1 before, /device:TPU:24 now
where the time goes in v3:
time: 108 us
  Pallas kernels  107 us (99%)
  local copies, waits for them, and re-layouts  1.67 us (2%)
    pallas_call x1, Pallas kernels, on_device(): pl.pallas_call(functools.partial(kernel, nz), out_shape=jax.ShapeDtypeStr...  107 us

profile of v3, /device:TPU:24, one launch (start us, length us, event | category | flops | bytes accessed | tf_op | source)
XLA Modules:
  0.0 108.3 jit_solution(8774835141978316247)
XLA Ops:
  0.0 106.6 %shard_map.64 = bf16[64,2048]{1,0:T(8,128)(2,1)} custom-call(bf16[64,2048]{1,0:T(8,128)(2,1)} %tok.1, bf16[2048,256]{1,0:T(8,128)(2,1)} %gate.1, bf16[2048,256]{1,0:T(8,128)(2,1)} %up.1, bf16[256,2048]{1,0:T(8,128)(2,1)} %down.1, s32[8,64]{1,0:T(8,128)} %bitcast.2, f32[8,64]{1,0:T(8,128)} %bitcast.3), custom_call_target="tpu_custom_call" | custom-call | flops 12884901888 | bytes 4194304 | tf_op jit(solution)/shard_map/pallas_call | solution.py:414
  106.6 1.7 %copy.8 = bf16[64,2048]{1,0:T(8,128)(2,1)} copy(bf16[64,2048]{1,0:T(8,128)(2,1)} %shard_map.64) | data formatting | bytes 524288

commit v4 on v3

--- a/solution.py
+++ b/solution.py
@@ -13,19 +13,27 @@
 MESH = pl.DeviceIdType.MESH
 
 
-def kernel(nz, tok, gate, up, down, ids_hbm, rw_hbm, out, tokbuf, rs, contrib, hid, gb, ub, wb, shr, shc, ids, rw, outbuf,
+def kernel(nz, tok, gate, up, down, ids_hbm, rw_hbm, out, tokbuf, rs, contrib, hid, gb, ub, wb, shr, shc, ids, rw,
+           pk, pk_back, pk_in, oh, oht,
            ag_send, ag_recv, rs_send, rs_recv, own_sem, sib_send, sib_recv, x_send, x_recv, fw_send, fw_recv,
-           sh_send, sh_recv, in_sem, out_sem):
+           sh_send, sh_recv, in_sem):
     nh = nz // 2
-    order = [0] + [s for t in range(1, nh) for s in (t, nz - t)] + [nh]
-    early, middle, late, last = order[:nh], order[nh:nh + nh // 2], order[nh + nh // 2:-1], order[-1:]
+    full = (nh - 1, nh - 2)
+    packer, packed = (nh - 1, nh + 2), (nh, nh + 1)
+    order = [0] + [s for t in range(1, nh - 1) for s in (t, nz - t)] + [nh - 1]
+    early, middle, late = order[:nh], order[nh:nh + nh // 2], order[nh + nh // 2:]
     place, tiles, row = {}, {}, 0
-    for name, slots, halves in (("A0", early, (0,)), ("A1", early, (1,)), ("B", middle, (0, 1)), ("C", late, (0, 1)), ("D", last, (0, 1))):
-        tiles[name] = (row, len(slots) * len(halves) * HALF)
-        for half in halves:
-            for slot in slots:
-                place[half, slot] = row
-                row += HALF
+    for name, blocks in (
+        ("A0", [(0, slot) for slot in early]),
+        ("A1", [(1, slot) for slot in early]),
+        ("B", [(half, slot) for half in range(2) for slot in middle]),
+        ("C", [(half, slot) for slot in late for half in range(2)] + [packed[1]]),
+        ("D", [packed[0]]),
+    ):
+        tiles[name] = (row, len(blocks) * HALF)
+        for block in blocks:
+            place[block] = row
+            row += HALF
     features = tok.shape[1]
     hdev = gate.shape[1]
     d = lax.axis_index("dp")
@@ -35,8 +43,9 @@
     x_lo = lax.rem(e // 2, 2)
     x_hi = lax.rem(d, 2)
     n_exp = 4 * nz
-    zp = lax.rem(e + 4, n_exp)
-    zm = lax.rem(e + n_exp - 4, n_exp)
+    way = 1 - 2 * core
+    targets = (lax.rem(e + n_exp + 4 * way, n_exp), lax.rem(e + n_exp - 4 * way, n_exp))
+    next_plane = (lax.rem(z + nz + way, nz), lax.rem(z + nz - way, nz))
     sib = e + 1 - 2 * core
     xq = e + 2 - 4 * x_lo
     d_other = d + 1 - 2 * x_hi
@@ -45,18 +54,12 @@
         return {"dp": dd, "expert": ee}
 
     barrier = pltpu.get_barrier_semaphore()
-    peers = [(d, zp), (d, zm), (d, xq), (d_other, xq), (d, sib)]
+    peers = [(d, targets[0]), (d, targets[1]), (d, xq), (d_other, xq), (d, sib)]
     for dd, ee in peers:
         pl.semaphore_signal(barrier, inc=1, device_id=dev(dd, ee), device_id_type=MESH)
 
-    def ag_has(dirn, t, q):
-        return t < nh or (t == nh and q == dirn)
-
     def ag_copy(dirn, t, half, q):
-        if dirn == 0:
-            src_slot, dst_slot, target = t - 1, t, zp
-        else:
-            src_slot, dst_slot, target = (nz - t + 1) % nz, nz - t, zm
+        src_slot, dst_slot = (t - 1, t) if dirn == 0 else ((nz - t + 1) % nz, nz - t)
         if t == 1:
             src = tok.at[pl.ds(half * HALF + q * Q, Q), :]
         else:
@@ -67,41 +70,55 @@
             dst_ref=tokbuf.at[pl.ds(place[half, dst_slot] + q * Q, Q), :],
             send_sem=ag_send.at[dirn, t - 1, i],
             recv_sem=ag_recv.at[dirn, t - 1, i],
-            device_id=dev(d, target),
+            device_id=dev(d, targets[dirn]),
+            device_id_type=MESH,
+        )
+
+    def pack_copy(dirn):
+        return pltpu.make_async_remote_copy(
+            src_ref=pk.at[dirn],
+            dst_ref=tokbuf.at[pl.ds(place[packed[dirn]], CAP), :],
+            send_sem=ag_send.at[dirn, full[dirn], 0],
+            recv_sem=ag_recv.at[dirn, full[dirn], 0],
+            device_id=dev(d, targets[dirn]),
             device_id_type=MESH,
         )
 
     def ag_first(half):
         for q in range(2):
             for dirn in range(2):
-                if ag_has(dirn, 1, q):
-                    ag_copy(dirn, 1, half, q).start()
-
-    def rs_has(dirn, t, q):
-        return t > 1 or q == 1 - dirn
+                ag_copy(dirn, 1, half, q).start()
+
+    def back_copy(dirn):
+        return pltpu.make_async_remote_copy(
+            src_ref=pk_back.at[dirn],
+            dst_ref=pk_in.at[dirn],
+            send_sem=rs_send.at[dirn, 0, 0],
+            recv_sem=rs_recv.at[dirn, 0, 0],
+            device_id=dev(d, targets[1 - dirn]),
+            device_id_type=MESH,
+        )
+
+    def rs_slots(dirn, t):
+        return (nh + 1 - t, nh - t) if dirn == 0 else (nh + t, nh + 1 + t)
 
     def rs_copy(dirn, t, half, q):
-        if dirn == 0:
-            src_slot, dst_slot, target = nh - 1 + t, nh + t, zp
-        else:
-            src_slot, dst_slot, target = nh + 1 - t, nh - t, zm
+        src_slot, dst_slot = rs_slots(dirn, t)
         i = half * 2 + q
         return pltpu.make_async_remote_copy(
             src_ref=rs.at[half, src_slot, pl.ds(q * Q, Q), :],
             dst_ref=rs.at[half, dst_slot, pl.ds(q * Q, Q), :],
             send_sem=rs_send.at[dirn, t - 1, i],
             recv_sem=rs_recv.at[dirn, t - 1, i],
-            device_id=dev(d, target),
+            device_id=dev(d, targets[1 - dirn]),
             device_id_type=MESH,
         )
 
     def rs_hop(dirn, t, half, q):
-        if not rs_has(dirn, t, q):
-            return
-        slot = nh - 1 + t if dirn == 0 else nh + 1 - t
+        slot = rs_slots(dirn, t)[0]
         rows = pl.ds(q * Q, Q)
         total = contrib[pl.ds(place[half, slot] + q * Q, Q), :]
-        if t > 1 and rs_has(dirn, t - 1, q):
+        if t > 2:
             rs_copy(dirn, t - 1, half, q).wait_recv()
             total = total + rs[half, slot, rows, :].astype(jnp.float32)
         rs[half, slot, rows, :] = total.astype(jnp.bfloat16)
@@ -110,15 +127,10 @@
     def rs_last(half, q):
         rows = pl.ds(q * Q, Q)
         rs_copy(0, nh, half, q).wait_recv()
-        rs_copy(1, nh, half, q).wait_recv()
+        rs_copy(1, nh - 1, half, q).wait_recv()
         total = contrib[pl.ds(place[half, 0] + q * Q, Q), :]
         total = total + rs[half, 0, rows, :].astype(jnp.float32) + rs[half, nz, rows, :].astype(jnp.float32)
-        outbuf[pl.ds(half * HALF + q * Q, Q), :] = total.astype(jnp.bfloat16)
-        out_copy(half, q).start()
-
-    def out_copy(half, q):
-        rows = pl.ds(half * HALF + q * Q, Q)
-        return pltpu.make_async_copy(outbuf.at[rows, :], out.at[rows, :], out_sem.at[half * 2 + q])
+        out[pl.ds(half * HALF + q * Q, Q), :] = total.astype(jnp.bfloat16)
 
     sources = (gate, up, down)
 
@@ -179,14 +191,11 @@
         return t < nh or dirn == 0
 
     def share_copy(dirn, t):
-        if dirn == 0:
-            src_slot, dst_slot, target = t - 1, t, zp
-        else:
-            src_slot, dst_slot, target = (nz - t + 1) % nz, nz - t, zm
+        src_slot, dst_slot = (t - 1, t) if dirn == 0 else ((nz - t + 1) % nz, nz - t)
         return pltpu.make_async_remote_copy(
             src_ref=shr.at[src_slot], dst_ref=shr.at[dst_slot],
             send_sem=sh_send.at[dirn, t - 1], recv_sem=sh_recv.at[dirn, t - 1],
-            device_id=dev(d, target), device_id_type=MESH)
+            device_id=dev(d, targets[dirn]), device_id_type=MESH)
 
     def make_shares():
         experts = lax.broadcasted_iota(jnp.int32, (nz, 64), 0)
@@ -212,6 +221,46 @@
             column = jnp.sum(jnp.where(diag, mine, 0.0), axis=1, keepdims=True)
             for half in range(2):
                 shc[pl.ds(place[half, slot], HALF), :] = column[half * HALF:(half + 1) * HALF]
+
+    def chosen(slot, expert):
+        both = shr[slot, pl.ds(lax.rem(expert, 8), 1), :]
+        share = jnp.where(expert >= 8, both[:, 64:], both[:, :64])
+        kept = jnp.where(share > 0.0, 1.0, 0.0)
+        before = lax.broadcasted_iota(jnp.int32, (64, 64), 0) < lax.broadcasted_iota(jnp.int32, (64, 64), 1)
+        place_of = jnp.dot(jnp.broadcast_to(kept, (16, 64)).astype(jnp.bfloat16), jnp.where(before, 1.0, 0.0).astype(jnp.bfloat16),
+                           preferred_element_type=jnp.float32)[:1]
+        place_of = jnp.where(kept > 0.0, place_of, -1.0)
+        slots = lax.broadcasted_iota(jnp.int32, (CAP, 64), 0).astype(jnp.float32)
+        return share, place_of, jnp.where(slots == place_of, 1.0, 0.0)
+
+    def prepare(dirn):
+        share, place_of, pick = chosen(packer[dirn], next_plane[dirn])
+        oh[dirn, :, :] = pick.astype(jnp.bfloat16)
+        diag = lax.broadcasted_iota(jnp.int32, (64, 64), 0) == lax.broadcasted_iota(jnp.int32, (64, 64), 1)
+        column = jnp.sum(jnp.where(diag, place_of, 0.0), axis=1, keepdims=True)
+        slots = lax.broadcasted_iota(jnp.int32, (64, CAP), 1).astype(jnp.float32)
+        oht[dirn, :, :] = jnp.where(slots == column, 1.0, 0.0).astype(jnp.bfloat16)
+
+    def pack(dirn):
+        block = tokbuf[pl.ds(place[0, packer[dirn]], 2 * HALF), :]
+        pk[dirn, :, :] = jnp.dot(oh[dirn], block, preferred_element_type=jnp.float32).astype(jnp.bfloat16)
+        pack_copy(dirn).start()
+
+    def take_packed_shares(dirn):
+        share, place_of, pick = chosen(packed[dirn], z)
+        shc[pl.ds(place[packed[dirn]], CAP), :] = jnp.sum(pick * share, axis=1, keepdims=True)
+
+    def send_back(dirn):
+        pk_back[dirn, :, :] = contrib[pl.ds(place[packed[dirn]], CAP), :].astype(jnp.bfloat16)
+        back_copy(dirn).start()
+
+    def unpack(dirn):
+        back_copy(dirn).wait_recv()
+        rows = pl.ds(place[0, packer[dirn]], 2 * HALF)
+        contrib[rows, :] = contrib[rows, :] + jnp.dot(oht[dirn], pk_in[dirn], preferred_element_type=jnp.float32)
+        for half in range(2):
+            for q in range(2):
+                rs_hop(dirn, 2, half, q)
 
     def hidden(m, role):
         rows = pl.ds(*tiles[m])
@@ -253,9 +302,9 @@
 
     def spread(half, t, q):
         for dirn in range(2):
-            if ag_has(dirn, t, q):
+            if t <= full[dirn]:
                 ag_copy(dirn, t, half, q).wait_recv()
-            if t < nh and ag_has(dirn, t + 1, q):
+            if t + 1 <= full[dirn]:
                 ag_copy(dirn, t + 1, half, q).start()
 
     def spread_shares(t):
@@ -325,41 +374,49 @@
                 spread(half, t, q)
                 if half == 0 and q == 1:
                     spread_shares(t)
+                    for dirn in range(2):
+                        if t == full[dirn]:
+                            prepare(dirn)
+                for dirn in range(2):
+                    if (t, half, q) == (full[dirn], 1, 1):
+                        pack(dirn)
                 step(t + 0.1 * (2 * half + q))
     while copies or products:
         step(nh)
 
+    pack_copy(1).wait_recv()
     for role in range(4):
         hidden("C", role)
     arrive_down()
     take_shares(late)
+    take_packed_shares(1)
     for n in range(4):
         project("C", n)
-    for half in range(2):
-        rs_hop(0, 2, half, 0)
-        rs_hop(1, 2, half, 1)
+    send_back(1)
+    spread_shares(nh)
+    pack_copy(0).wait_recv()
+    for role in range(4):
+        hidden("D", role)
+    take_packed_shares(0)
+    for n in range(4):
+        project("D", n)
+    send_back(0)
+    unpack(1)
     for n in range(4):
         project("B", n)
-    for half in range(2):
-        for q in range(2):
-            spread(half, nh, q)
-    spread_shares(nh)
-    for role in range(4):
-        hidden("D", role)
-    take_shares(last)
-    for n in range(4):
-        project("D", n)
-    for half in range(2):
-        rs_hop(0, 1, half, 1)
-        rs_hop(1, 1, half, 0)
+    unpack(0)
 
     def sent():
         for half in range(2):
             for tt in range(1, nh + 1):
                 for q in range(2):
                     for dirn in range(2):
-                        if ag_has(dirn, tt, q):
+                        if tt <= full[dirn]:
                             ag_copy(dirn, tt, half, q).wait_send()
+
+        for dirn in range(2):
+            pack_copy(dirn).wait_send()
+            back_copy(dirn).wait_send()
 
     def weights_sent():
         for i in range(3):
@@ -379,15 +436,13 @@
     products.append((5, sent))
     products.append((5, weights_sent))
 
-    for t in range(2, nh + 1):
+    for t in range(3, nh + 1):
         for half in range(2):
-            if t < nh:
-                rs_hop(0, t + 1, half, 0)
-                rs_hop(1, t + 1, half, 1)
-            step(t)
-            rs_hop(0, t, half, 1)
-            rs_hop(1, t, half, 0)
-            step(t)
+            for q in range(2):
+                if t < nh:
+                    rs_hop(1, t, half, q)
+                step(t)
+                rs_hop(0, t, half, q)
     for half in range(2):
         for q in range(2):
             rs_last(half, q)
@@ -395,11 +450,8 @@
         for t in range(1, nh + 1):
             for q in range(2):
                 for dirn in range(2):
-                    if rs_has(dirn, t, q):
+                    if 1 < t <= nh - dirn:
                         rs_copy(dirn, t, half, q).wait_send()
-    for half in range(2):
-        for q in range(2):
-            out_copy(half, q).wait()
 
 
 def solution(mesh):
@@ -413,9 +465,9 @@
         flops = 2 * rows * nz * features * 4 * hdev * 3
         return pl.pallas_call(
             functools.partial(kernel, nz),
-            out_shape=jax.ShapeDtypeStruct((rows, features), jnp.bfloat16),
+            out_shape=pltpu.VMEM((rows, features), jnp.bfloat16),
             in_specs=[pl.BlockSpec(memory_space=pl.ANY)] * 6,
-            out_specs=pl.BlockSpec(memory_space=pl.ANY),
+            out_specs=pl.BlockSpec(memory_space=pltpu.VMEM),
             scratch_shapes=[
                 pltpu.VMEM((nz * rows, features), jnp.bfloat16),
                 pltpu.VMEM((2, nz + 1, HALF, features), jnp.bfloat16),
@@ -428,7 +480,11 @@
                 pltpu.VMEM((nz * rows, 1), jnp.float32),
                 pltpu.VMEM((ids.shape[1], rows), jnp.int32),
                 pltpu.VMEM((ids.shape[1], rows), jnp.float32),
-                pltpu.VMEM((rows, features), jnp.bfloat16),
+                pltpu.VMEM((2, CAP, features), jnp.bfloat16),
+                pltpu.VMEM((2, CAP, features), jnp.bfloat16),
+                pltpu.VMEM((2, CAP, features), jnp.bfloat16),
+                pltpu.VMEM((2, CAP, rows), jnp.bfloat16),
+                pltpu.VMEM((2, rows, CAP), jnp.bfloat16),
                 dma((2, nh, 4)),
                 dma((2, nh, 4)),
                 dma((2, nh, 4)),
@@ -443,7 +499,6 @@
                 dma((2, nh)),
                 dma((2, nh)),
                 dma((2,)),
-                dma((4,)),
             ],
             compiler_params=pltpu.CompilerParams(
                 collective_id=0, has_side_effects=True, vmem_limit_bytes=56 * 1024 * 1024

time: 108 us -> 104 us (0.963)
  the two profiles are of different devices: /device:TPU:24 before, /device:TPU:1 now
where the time goes in v4:
time: 104 us
  Pallas kernels  104 us (100%)
    pallas_call x1, Pallas kernels, on_device(): pl.pallas_call(functools.partial(kernel, nz), out_shape=pltpu.VMEM((rows,...  104 us

profile of v4, /device:TPU:1, one launch (start us, length us, event | category | flops | bytes accessed | tf_op | source)
XLA Modules:
  0.0 104.3 jit_solution(7285618181769511731)
XLA Ops:
  0.0 103.6 %shard_map.64 = bf16[64,2048]{1,0:T(8,128)(2,1)S(1)} custom-call(bf16[64,2048]{1,0:T(8,128)(2,1)} %tok.1, bf16[2048,256]{1,0:T(8,128)(2,1)} %gate.1, bf16[2048,256]{1,0:T(8,128)(2,1)} %up.1, bf16[256,2048]{1,0:T(8,128)(2,1)} %down.1, s32[8,64]{1,0:T(8,128)} %bitcast.2, f32[8,64]{1,0:T(8,128)} %bitcast.3), custom_call_target="tpu_custom_call" | custom-call | flops 12884901888 | bytes 4194304 | tf_op jit(solution)/shard_map/pallas_call | solution.py:466
  103.6 0.7 copy.8

commit v5 on v4

--- a/solution.py
+++ b/solution.py
@@ -10,6 +10,7 @@
 CAP = 32
 Q = 16
 HALF = 32
+PIECES = 4
 MESH = pl.DeviceIdType.MESH
 
 
@@ -27,8 +28,8 @@
         ("A0", [(0, slot) for slot in early]),
         ("A1", [(1, slot) for slot in early]),
         ("B", [(half, slot) for half in range(2) for slot in middle]),
-        ("C", [(half, slot) for slot in late for half in range(2)] + [packed[1]]),
-        ("D", [packed[0]]),
+        ("C", [(half, packer[1]) for half in range(2)] + [packed[1]]),
+        ("D", [(half, packer[0]) for half in range(2)] + [packed[0]]),
     ):
         tiles[name] = (row, len(blocks) * HALF)
         for block in blocks:
@@ -74,12 +75,15 @@
             device_id_type=MESH,
         )
 
-    def pack_copy(dirn):
-        return pltpu.make_async_remote_copy(
-            src_ref=pk.at[dirn],
-            dst_ref=tokbuf.at[pl.ds(place[packed[dirn]], CAP), :],
-            send_sem=ag_send.at[dirn, full[dirn], 0],
-            recv_sem=ag_recv.at[dirn, full[dirn], 0],
+    width = features // PIECES
+
+    def pack_copy(dirn, n):
+        cols = pl.ds(n * width, width)
+        return pltpu.make_async_remote_copy(
+            src_ref=pk.at[dirn, :, cols],
+            dst_ref=tokbuf.at[pl.ds(place[packed[dirn]], CAP), cols],
+            send_sem=ag_send.at[dirn, full[dirn], n],
+            recv_sem=ag_recv.at[dirn, full[dirn], n],
             device_id=dev(d, targets[dirn]),
             device_id_type=MESH,
         )
@@ -89,12 +93,13 @@
             for dirn in range(2):
                 ag_copy(dirn, 1, half, q).start()
 
-    def back_copy(dirn):
-        return pltpu.make_async_remote_copy(
-            src_ref=pk_back.at[dirn],
-            dst_ref=pk_in.at[dirn],
-            send_sem=rs_send.at[dirn, 0, 0],
-            recv_sem=rs_recv.at[dirn, 0, 0],
+    def back_copy(dirn, n):
+        cols = pl.ds(n * width, width)
+        return pltpu.make_async_remote_copy(
+            src_ref=pk_back.at[dirn, :, cols],
+            dst_ref=pk_in.at[dirn, :, cols],
+            send_sem=rs_send.at[dirn, 0, n],
+            recv_sem=rs_recv.at[dirn, 0, n],
             device_id=dev(d, targets[1 - dirn]),
             device_id_type=MESH,
         )
@@ -123,6 +128,8 @@
             total = total + rs[half, slot, rows, :].astype(jnp.float32)
         rs[half, slot, rows, :] = total.astype(jnp.bfloat16)
         rs_copy(dirn, t, half, q).start()
+        if t > 3:
+            rs_copy(dirn, t - 2, half, q).wait_send()
 
     def rs_last(half, q):
         rows = pl.ds(q * Q, Q)
@@ -242,22 +249,31 @@
         oht[dirn, :, :] = jnp.where(slots == column, 1.0, 0.0).astype(jnp.bfloat16)
 
     def pack(dirn):
-        block = tokbuf[pl.ds(place[0, packer[dirn]], 2 * HALF), :]
-        pk[dirn, :, :] = jnp.dot(oh[dirn], block, preferred_element_type=jnp.float32).astype(jnp.bfloat16)
-        pack_copy(dirn).start()
+        for n in range(PIECES):
+            cols = pl.ds(n * width, width)
+            block = tokbuf[pl.ds(place[0, packer[dirn]], 2 * HALF), cols]
+            pk[dirn, :, cols] = jnp.dot(oh[dirn], block, preferred_element_type=jnp.float32).astype(jnp.bfloat16)
+            pack_copy(dirn, n).start()
+
+    def packed_arrived(dirn):
+        for n in range(PIECES):
+            pack_copy(dirn, n).wait_recv()
 
     def take_packed_shares(dirn):
         share, place_of, pick = chosen(packed[dirn], z)
         shc[pl.ds(place[packed[dirn]], CAP), :] = jnp.sum(pick * share, axis=1, keepdims=True)
 
-    def send_back(dirn):
-        pk_back[dirn, :, :] = contrib[pl.ds(place[packed[dirn]], CAP), :].astype(jnp.bfloat16)
-        back_copy(dirn).start()
+    def send_back(dirn, n):
+        cols = pl.ds(n * width, width)
+        pk_back[dirn, :, cols] = contrib[pl.ds(place[packed[dirn]], CAP), cols].astype(jnp.bfloat16)
+        back_copy(dirn, n).start()
 
     def unpack(dirn):
-        back_copy(dirn).wait_recv()
         rows = pl.ds(place[0, packer[dirn]], 2 * HALF)
-        contrib[rows, :] = contrib[rows, :] + jnp.dot(oht[dirn], pk_in[dirn], preferred_element_type=jnp.float32)
+        for n in range(PIECES):
+            back_copy(dirn, n).wait_recv()
+            cols = pl.ds(n * width, width)
+            contrib[rows, cols] = contrib[rows, cols] + jnp.dot(oht[dirn], pk_in[dirn, :, cols], preferred_element_type=jnp.float32)
         for half in range(2):
             for q in range(2):
                 rs_hop(dirn, 2, half, q)
@@ -271,7 +287,6 @@
 
     def project(m, n):
         rows = pl.ds(*tiles[m])
-        width = features // 4
         cols = slice(n * width, (n + 1) * width)
         acc = jnp.dot(hid[rows, :], wb[:, cols], preferred_element_type=jnp.float32)
         contrib[rows, cols] = acc * shc[rows, :]
@@ -384,57 +399,58 @@
     while copies or products:
         step(nh)
 
-    pack_copy(1).wait_recv()
+    take_shares(late)
+    take_packed_shares(1)
+    arrive_down()
+    packed_arrived(1)
     for role in range(4):
         hidden("C", role)
-    arrive_down()
-    take_shares(late)
-    take_packed_shares(1)
-    for n in range(4):
+    for n in range(PIECES):
         project("C", n)
-    send_back(1)
+        send_back(1, n)
     spread_shares(nh)
-    pack_copy(0).wait_recv()
+    take_packed_shares(0)
+    packed_arrived(0)
     for role in range(4):
         hidden("D", role)
-    take_packed_shares(0)
-    for n in range(4):
+    for n in range(PIECES):
         project("D", n)
-    send_back(0)
+        send_back(0, n)
     unpack(1)
-    for n in range(4):
+    for n in range(PIECES):
         project("B", n)
     unpack(0)
 
-    def sent():
+    done = []
+    for tt in range(1, nh + 1):
         for half in range(2):
-            for tt in range(1, nh + 1):
-                for q in range(2):
-                    for dirn in range(2):
-                        if tt <= full[dirn]:
-                            ag_copy(dirn, tt, half, q).wait_send()
-
+            for q in range(2):
+                for dirn in range(2):
+                    if tt <= full[dirn]:
+                        done.append(ag_copy(dirn, tt, half, q))
         for dirn in range(2):
-            pack_copy(dirn).wait_send()
-            back_copy(dirn).wait_send()
-
-    def weights_sent():
-        for i in range(3):
-            for k in range(4):
-                sib_copy(i, k).wait_send()
-                fw_copy(i, k).wait_send()
-            for side in range(2):
-                x_copy(i, side).wait_send()
-        for tt in range(1, nh + 1):
-            for dirn in range(2):
-                if share_has(dirn, tt):
-                    share_copy(dirn, tt).wait_send()
+            if share_has(dirn, tt):
+                done.append(share_copy(dirn, tt))
+    for dirn in range(2):
+        for n in range(PIECES):
+            done.append(pack_copy(dirn, n))
+            done.append(back_copy(dirn, n))
+    for i in range(3):
+        for k in range(4):
+            done.append(sib_copy(i, k))
+            done.append(fw_copy(i, k))
+        for side in range(2):
+            done.append(x_copy(i, side))
+
+    def sent(copies):
+        for copy in copies:
+            copy.wait_send()
 
     for half in range(2):
         for n in range(4):
             products.append((2, project, ("A0", "A1")[half], n))
-    products.append((5, sent))
-    products.append((5, weights_sent))
+    for i in range(0, len(done), 8):
+        products.append((4, sent, done[i:i + 8]))
 
     for t in range(3, nh + 1):
         for half in range(2):
@@ -446,12 +462,13 @@
     for half in range(2):
         for q in range(2):
             rs_last(half, q)
+    while products:
+        step(nh + 1)
     for half in range(2):
-        for t in range(1, nh + 1):
-            for q in range(2):
-                for dirn in range(2):
-                    if 1 < t <= nh - dirn:
-                        rs_copy(dirn, t, half, q).wait_send()
+        for q in range(2):
+            for dirn in range(2):
+                for t in range(full[dirn], full[dirn] + 2):
+                    rs_copy(dirn, t, half, q).wait_send()
 
 
 def solution(mesh):

time: 104 us -> 104 us (level)
  no operation moved by 1% of the time
where the time goes in v5:
time: 104 us
  Pallas kernels  103 us (99%)
    pallas_call x1, Pallas kernels, on_device(): pl.pallas_call(functools.partial(kernel, nz), out_shape=pltpu.VMEM((rows,...  103 us

profile of v5, /device:TPU:1, one launch (start us, length us, event | category | flops | bytes accessed | tf_op | source)
XLA Modules:
  0.0 103.9 jit_solution(9835262372810729013)
XLA Ops:
  0.0 103.2 %shard_map.64 = bf16[64,2048]{1,0:T(8,128)(2,1)S(1)} custom-call(bf16[64,2048]{1,0:T(8,128)(2,1)} %tok.1, bf16[2048,256]{1,0:T(8,128)(2,1)} %gate.1, bf16[2048,256]{1,0:T(8,128)(2,1)} %up.1, bf16[256,2048]{1,0:T(8,128)(2,1)} %down.1, s32[8,64]{1,0:T(8,128)} %bitcast.2, f32[8,64]{1,0:T(8,128)} %bitcast.3), custom_call_target="tpu_custom_call" | custom-call | flops 12884901888 | bytes 4194304 | tf_op jit(solution)/shard_map/pallas_call | solution.py:483
  103.2 0.7 copy.8

commit v6 on v5

--- a/solution.py
+++ b/solution.py
@@ -10,7 +10,7 @@
 CAP = 32
 Q = 16
 HALF = 32
-PIECES = 4
+PIECES = 2
 MESH = pl.DeviceIdType.MESH
 
 
@@ -447,7 +447,7 @@
             copy.wait_send()
 
     for half in range(2):
-        for n in range(4):
+        for n in range(PIECES):
             products.append((2, project, ("A0", "A1")[half], n))
     for i in range(0, len(done), 8):
         products.append((4, sent, done[i:i + 8]))

time: 104 us -> 104 us (level)
  no operation moved by 1% of the time
where the time goes in v6:
time: 104 us
  Pallas kernels  103 us (99%)
    pallas_call x1, Pallas kernels, on_device(): pl.pallas_call(functools.partial(kernel, nz), out_shape=pltpu.VMEM((rows,...  103 us

profile of v6, /device:TPU:1, one launch (start us, length us, event | category | flops | bytes accessed | tf_op | source)
XLA Modules:
  0.0 103.6 jit_solution(17946198304860626998)
XLA Ops:
  0.0 102.9 %shard_map.64 = bf16[64,2048]{1,0:T(8,128)(2,1)S(1)} custom-call(bf16[64,2048]{1,0:T(8,128)(2,1)} %tok.1, bf16[2048,256]{1,0:T(8,128)(2,1)} %gate.1, bf16[2048,256]{1,0:T(8,128)(2,1)} %up.1, bf16[256,2048]{1,0:T(8,128)(2,1)} %down.1, s32[8,64]{1,0:T(8,128)} %bitcast.2, f32[8,64]{1,0:T(8,128)} %bitcast.3), custom_call_target="tpu_custom_call" | custom-call | flops 12884901888 | bytes 4194304 | tf_op jit(solution)/shard_map/pallas_call | solution.py:483
  102.9 0.7 copy.8
